TPU v7x, 32 devices: a whole 2x2x4 slice. The times are simulated.
32 devices in a mesh: particle: 4 (over z), space: 8 (over y, x, core).
Axes of the slice: x: 2, y: 2, z: 4, core: 2. Of those that a mesh axis runs over, the one named last changes fastest.
Arguments:
- stream: float32 [4, 512, 2048], P('particle', 'space'), may hold values from -6 to 6
- depth_field: float32 [512, 2048], P('space'), may hold values from 0.5 to 4
- obs_col: int32 [512, 16], P('space'), may hold values from 0 to 2047
- obs_val: float32 [512, 16], P('space'), may hold values from -6 to 6
- obs_weight: float32 [512, 16], P('space'), may hold values from 0.1 to 1
- log_weight: float32 [4], P('particle'), may hold values from -6144 to 6144
- target: float32 [1], replicated, may hold values from 0 to 2048
- spectrum: float32 [512, 512], P('space'), may hold values from 1 to 10
- noise_coef: bfloat16 [4, 512, 512], P('particle', 'space'), may hold values from -6 to 6
- selection: int32 [2, 4], replicated, may hold values from 0 to 1
Outputs:
- analysis: float32 [4, 512, 2048], P('particle', 'space')
- misfit_out: float32 [4], P('particle')
All inputs are finite; a program needn't handle non-finite values.
Results may differ from a plain program's by a relative error of at most 0.0003.
The roundings to bfloat16 on the way count: a program that leaves them out, or rounds other values in their place, can miss the bound.
Values may be sent and summed in bfloat16 or wider, within the bound.
A program may use at most 64 MiB of HBM per device.

v0:
```python
import math

import jax
import jax.numpy as jnp
from jax import lax
from jax.sharding import PartitionSpec as P

ITERS = 2


STRETCH = 0.05
RELAX_RATE = 0.8
NOISE_AMP = 0.3


def extended(cells, sides, width):
    for axis, dim in sides:
        count = lax.axis_size(axis)
        ends = count - 1
        head = lax.slice_in_dim(cells, 0, width, axis=dim)
        tail = lax.slice_in_dim(cells, cells.shape[dim] - width, cells.shape[dim], axis=dim)
        cells = jnp.concatenate(
            [
                lax.ppermute(tail, axis, [(i, (i + 1) % count) for i in range(ends)]),
                cells,
                lax.ppermute(head, axis, [((i + 1) % count, i) for i in range(ends)]),
            ],
            axis=dim,
        )
    return cells


def swapped(value, axis, bit):
    mask = 2**bit
    pairs = [(source, source ^ mask) for source in range(lax.axis_size(axis))]
    return lax.ppermute(value, axis, pairs)


def tables(extent, half_modes):
    cell_index = jnp.arange(extent, dtype=jnp.int32)[:, None]
    frequency = jnp.arange(half_modes + 1, dtype=jnp.int32)[None, :]
    angles = (cell_index * frequency % extent).astype(jnp.float32) * (2.0 * math.pi / extent)
    cosines = jnp.cos(angles).astype(jnp.bfloat16)
    sines = jnp.sin(angles[:, 1:half_modes]).astype(jnp.bfloat16)
    return jnp.concatenate([cosines, sines], axis=1)


def compare_obs(grid_field, obs_col, obs_val, obs_weight):
    index_grid = jnp.broadcast_to(obs_col, grid_field.shape[:-1] + obs_col.shape[-1:])
    seen_vals = jnp.take_along_axis(grid_field, index_grid, axis=-1)
    mismatch_vals = obs_val - seen_vals
    return (mismatch_vals, 0.5 * jnp.sum(obs_weight * mismatch_vals * mismatch_vals, axis=(-2, -1)))


def spread_obs(weighted_miss, obs_col, columns):
    row_index = jnp.broadcast_to(
        jnp.arange(obs_col.shape[0], dtype=jnp.int32)[:, None], obs_col.shape
    )
    return (
        jnp.zeros((obs_col.shape[0], columns), jnp.float32)
        .at[row_index, obs_col]
        .add(weighted_miss)
    )


def operate_band(grid_field, screening):
    padded = extended(grid_field, (("space", 1),), 1)
    return (
        padded[:, 2:]
        + padded[:, :-2]
        + jnp.roll(grid_field, 1, axis=2)
        + jnp.roll(grid_field, -1, axis=2)
        - (4.0 + screening) * grid_field
    )


def relax_all(base, increment, depth_field):
    screening = STRETCH / depth_field
    pv_target = operate_band(base, screening) + increment
    relaxed = base + increment
    for sweep_index in range(ITERS):
        relaxed = relaxed + RELAX_RATE * (operate_band(relaxed, screening) - pv_target) / (
            4.0 + screening
        )
    return relaxed


def per_device(
    stream,
    depth_field,
    obs_col,
    obs_val,
    obs_weight,
    log_weight,
    target,
    spectrum,
    noise_coef,
    selection,
):
    members = stream.shape[0]
    band_rows = stream.shape[1]
    columns = stream.shape[2]
    n_modes = spectrum.shape[1]
    total_rows = band_rows * lax.axis_size("space")
    x_table = tables(columns, n_modes // 2)
    y_table = tables(total_rows, n_modes // 2)
    norm_factor = 4.0 / (columns * total_rows)
    mismatch_vals, misfit_part = compare_obs(stream, obs_col, obs_val, obs_weight)
    misfit = lax.psum(misfit_part, "space")
    gradient = jax.vmap(lambda weighted_miss: spread_obs(weighted_miss, obs_col, columns))(
        obs_weight * mismatch_vals
    ).astype(jnp.bfloat16)
    row_modes = jnp.einsum(
        "prx,xk->pkr", gradient, x_table, preferred_element_type=jnp.float32
    ).astype(jnp.bfloat16)
    col_modes = lax.all_to_all(row_modes, "space", split_axis=1, concat_axis=2, tiled=True)
    coefficients = jnp.einsum("pky,ym->pkm", col_modes, y_table, preferred_element_type=jnp.float32)
    weighted = coefficients * (norm_factor * spectrum)
    energy_part = jnp.sum(coefficients * weighted, axis=(1, 2))
    energy = lax.psum(energy_part, "space")
    shaped = (jnp.sqrt(norm_factor * spectrum) * noise_coef.astype(jnp.float32)).astype(
        jnp.bfloat16
    )
    stacked = jnp.concatenate([weighted.astype(jnp.bfloat16), shaped], axis=0)
    inverted = jnp.einsum(
        "qkm,ym->qky", stacked, y_table, preferred_element_type=jnp.float32
    ).astype(jnp.bfloat16)
    band_modes = lax.all_to_all(inverted, "space", split_axis=2, concat_axis=1, tiled=True)
    pulled = jnp.einsum("qkr,xk->qrx", band_modes, x_table, preferred_element_type=jnp.float32)
    step_size = (misfit + log_weight - target[0]) / (energy + 1.0)
    increment = step_size[:, None, None] * pulled[:members] + NOISE_AMP * pulled[members:]
    island = lax.axis_index("particle")
    fields = relax_all(stream, increment, depth_field)
    for section_bit in range(selection.shape[0]):
        chosen = lax.dynamic_slice_in_dim(selection[section_bit], island * members, members)
        partner = swapped(fields, "particle", section_bit)
        fields = jnp.take(jnp.concatenate([fields, partner], axis=0), chosen, axis=0)
    final_miss, final_part = compare_obs(fields, obs_col, obs_val, obs_weight)
    misfit_out = lax.psum(final_part, "space")
    return (fields, misfit_out)


def solution(mesh):
    return jax.shard_map(
        per_device,
        mesh=mesh,
        in_specs=(
            P("particle", "space", None),
            P("space", None),
            P("space", None),
            P("space", None),
            P("space", None),
            P("particle"),
            P(),
            P("space", None),
            P("particle", "space", None),
            P(),
        ),
        out_specs=(P("particle", "space", None), P("particle")),
        check_vma=False,
    )
```

profile of v0, /device:TPU:0, one launch (start us, length us, event | category | flops | bytes accessed | tf_op | source)
XLA Modules:
  0.0 172.1 jit_solution(17163207104353408622)
XLA Ops:
  0.6 0.8 copy.28
  2.2 3.2 %fusion.2 = f32[2048,257]{1,0:T(8,128)} fusion(), kind=kLoop, calls=%fused_computation.8 | loop fusion | flops 7368704 | bytes 2105344 | tf_op jit(solution)/shard_map/mul | solution.py:42
  5.3 11.8 %cosine_convert_fusion = bf16[2048,257]{1,0:T(8,128)(2,1)S(1)} fusion(), kind=kLoop, calls=%fused_computation.9 | loop fusion | flops 7895040 | bytes 1052672 | tf_op jit(solution)/shard_map/convert_element_type | solution.py:43
  17.3 8.6 %gather_fusion = f32[1024]{0:T(1024)S(1)} fusion(f32[64,2048]{1,0:T(8,128)S(1)} %bitcast.89, s32[1024]{0:T(1024)S(1)} %reshape.159), kind=kCustom, calls=%fused_computation.clone | custom fusion | bytes 16384 | tf_op jit(solution)/shard_map/jit(take_along_axis)/gather | solution.py:50
  27.2 6.1 %scatter_custom_fusion = f32[131072]{0:T(1024)S(1)} fusion(s32[1024]{0:T(1024)S(1)} %reshape.136, f32[1024]{0:T(1024)S(1)} %reshape.138, f32[]{:T(128)} %constant.44.clone.1), kind=kCustom, calls=%fused_computation.79 | custom fusion | flops 1024 | bytes 524292
  33.4 8.4 %fusion.6 = bf16[2048,255]{1,0:T(8,128)(2,1)S(1)} fusion(f32[2048,257]{1,0:T(8,128)} %fusion.2), kind=kLoop, calls=%fused_computation.14 | loop fusion | flops 522240 | bytes 3133440 | tf_op jit(solution)/shard_map/convert_element_type | solution.py:44
  43.1 1.5 reduce.8
  45.3 5.2 %all-to-all-start = ((bf16[8,2,2048]{2,1,0:T(2,128)(2,1)}), bf16[8,2,2048]{2,1,0:T(2,128)(2,1)S(1)}, u32[]{:S(2)}, u32[]{:S(2)}) async-start(bf16[8,2,2048]{2,1,0:T(2,128)(2,1)} %reshape.175), calls=%async_computation | async-start | bytes 131072 | tf_op jit(solution)/shard_map/all_to_all | solution.py:116
  50.9 2.5 %fusion.42 = bf16[512,255]{1,0:T(8,128)(2,1)} fusion(f32[512,257]{1,0:T(8,128)S(1)} %fusion.12), kind=kLoop, calls=%fused_computation.70 | loop fusion | flops 130560 | bytes 783360 | tf_op jit(solution)/shard_map/convert_element_type | solution.py:44
  53.4 1.6 fusion.50
  55.1 3.6 %cosine_convert_fusion.1 = bf16[512,257]{1,0:T(8,128)(2,1)} fusion(), kind=kLoop, calls=%fused_computation.31 | loop fusion | flops 1973760 | bytes 263168 | tf_op jit(solution)/shard_map/convert_element_type | solution.py:43
  59.4 2.0 %multiply_reduce_fusion = (f32[]{:T(128)}, bf16[1,64,512]{2,1,0:T(8,128)(2,1)S(1)}) fusion(f32[64,512]{1,0:T(8,128)} %param.21, bf16[64,512]{1,0:T(8,128)(2,1)S(1)} %reshape.71, bf16[512,255]{1,0:T(8,128)(2,1)} %fusion.42, bf16[512,257]{1,0:T(8,128)(2,1)} %cosine_convert_fusion.1), kind=kOutput, calls=%fused_computation.86 | convolution fusion | flops 34766848 | bytes 786436 | tf_op jit(solution)/shard_map/pky,ym->pkm/dot_general | solution.py:117
  61.4 1.4 convolution_convert_fusion
  63.0 0.9 reshape.177
  63.9 4.2 %all-to-all-start.1 = ((bf16[8,2,4096]{2,1,0:T(2,128)(2,1)}), bf16[8,2,4096]{2,1,0:T(2,128)(2,1)S(1)}, u32[]{:S(2)}, u32[]{:S(2)}) async-start(bf16[8,2,4096]{2,1,0:T(2,128)(2,1)} %reshape.177), calls=%async_computation.1 | async-start | bytes 262144 | tf_op jit(solution)/shard_map/all_to_all | solution.py:128
  68.7 1.3 collective-permute-start.2
  70.0 3.6 %collective-permute-start.3 = (f32[1,1,2048]{2,1,0:T(1,128)}, f32[1,1,2048]{2,1,0:T(1,128)}, u32[]{:S(2)}, u32[]{:S(2)}) collective-permute-start(f32[1,1,2048]{2,1,0:T(1,128)} %get-tuple-element.28), channel_id=1, source_target_pairs={{0,1},{1,2},{2,3},{3,4},{4,5},{5,6},{6,7},{8,9},{9,10},{10,11},{11... | collective-permute-start | bytes 24584 | tf_op jit(solution)/shard_map/ppermute | solution.py:24
  75.6 15.0 %all-reduce = (f32[1]{0:T(128)}, f32[1]{0:T(128)}) all-reduce(f32[1]{0:T(128)} %bitcast.9, f32[1]{0:T(128)} %bitcast.13), channel_id=1, replica_groups=mesh['particle'=4,'space'=8] {'space'}, use_global_device_ids=true, to_apply=%region_1.3 | all-reduce | flops 2 | bytes 16 | tf_op jit(solution)/shard_map/psum | solution.py:109
  92.2 0.9 copy.36
  93.0 1.2 all_to_all.30
  94.2 0.8 fusion.7
  95.6 1.3 collective-permute-start
  96.9 3.0 %collective-permute-start.1 = (f32[1,1,2048]{2,1,0:T(1,128)S(1)}, f32[1,1,2048]{2,1,0:T(1,128)S(1)}, u32[]{:S(2)}, u32[]{:S(2)}) collective-permute-start(f32[1,1,2048]{2,1,0:T(1,128)S(1)} %get-tuple-element.38), channel_id=1, source_target_pairs={{0,1},{1,2},{2,3},{3,4},{4,5},{5,6},{6,7},{8,9},{9,10},{10,11},{11... | collective-permute-start | bytes 24584 | tf_op jit(solution)/shard_map/ppermute | solution.py:24
  100.7 1.4 fusion.40
  102.3 1.3 collective-permute-start.4
  103.6 3.0 %collective-permute-start.5 = (f32[1,1,2048]{2,1,0:T(1,128)S(1)}, f32[1,1,2048]{2,1,0:T(1,128)S(1)}, u32[]{:S(2)}, u32[]{:S(2)}) collective-permute-start(f32[1,1,2048]{2,1,0:T(1,128)S(1)} %get-tuple-element.26), channel_id=1, source_target_pairs={{0,1},{1,2},{2,3},{3,4},{4,5},{5,6},{6,7},{8,9},{9,10},{10,11},{11... | collective-permute-start | bytes 24584 | tf_op jit(solution)/shard_map/ppermute | solution.py:24
  107.9 1.6 collective-permute-start.6
  112.0 10.0 %collective-permute-done.6 = f32[1,64,2048]{2,1,0:T(8,128)S(1)} collective-permute-done((f32[1,64,2048]{2,1,0:T(8,128)S(1)}, f32[1,64,2048]{2,1,0:T(8,128)S(1)}, u32[]{:S(2)}, u32[]{:S(2)}) %collective-permute-start.6) | collective-permute-done | bytes 524320 | tf_op jit(solution)/shard_map/ppermute | solution.py:36
  122.1 2.7 %collective-permute-start.7 = (f32[1,64,2048]{2,1,0:T(8,128)S(1)}, f32[1,64,2048]{2,1,0:T(8,128)S(1)}, u32[]{:S(2)}, u32[]{:S(2)}) collective-permute-start(f32[1,64,2048]{2,1,0:T(8,128)S(1)} %fusion.19), channel_id=1, source_target_pairs={{0,16},{8,24},{16,0},{24,8},{1,17},{9,25},{17,1},{25,9},{2,18},{10... | collective-permute-start | bytes 1572872 | tf_op jit(solution)/shard_map/ppermute | solution.py:36
  126.7 22.0 %collective-permute-done.7 = f32[1,64,2048]{2,1,0:T(8,128)S(1)} collective-permute-done((f32[1,64,2048]{2,1,0:T(8,128)S(1)}, f32[1,64,2048]{2,1,0:T(8,128)S(1)}, u32[]{:S(2)}, u32[]{:S(2)}) %collective-permute-start.7) | collective-permute-done | bytes 524320 | tf_op jit(solution)/shard_map/ppermute | solution.py:36
  148.8 8.6 %gather_fusion.1 = f32[1024]{0:T(1024)S(1)} fusion(f32[64,2048]{1,0:T(8,128)S(1)} %bitcast.90, s32[1024]{0:T(1024)S(1)} %reshape.159), kind=kCustom, calls=%fused_computation.1.clone | custom fusion | bytes 16384 | tf_op jit(solution)/shard_map/jit(take_along_axis)/gather | solution.py:50
  158.8 13.3 %psum.23 = f32[1]{0:T(128)} all-reduce(f32[1]{0:T(128)} %bitcast.26), channel_id=1, replica_groups=mesh['particle'=4,'space'=8] {'space'}, use_global_device_ids=true, to_apply=%region_6.9 | all-reduce | flops 1 | bytes 8 | tf_op jit(solution)/shard_map/psum | solution.py:139
  (76 shorter events, 10.5 us)
Async XLA Ops:
  0.6 16.6 %copy-start = (f32[1,64,2048]{2,1,0:T(8,128)S(1)}, f32[1,64,2048]{2,1,0:T(8,128)}, u32[]{:S(2)}) copy-start(f32[1,64,2048]{2,1,0:T(8,128)} %param.14) | copy-start | bytes 1572868
  17.2 8.7 %copy-start.7 = (f32[64,16]{0,1:T(8,128)S(1)}, f32[64,16]{0,1:T(8,128)}, u32[]{:S(2)}) copy-start(f32[64,16]{0,1:T(8,128)} %param.18) | copy-start | bytes 12292
  17.2 8.8 %copy-start.8 = (f32[64,16]{0,1:T(8,128)S(1)}, f32[64,16]{0,1:T(8,128)}, u32[]{:S(2)}) copy-start(f32[64,16]{0,1:T(8,128)} %param.17) | copy-start | bytes 12292
  17.2 9.6 %copy-start.10 = (s32[2]{0:T(128)S(1)}, s32[2]{0:T(128)}, u32[]{:S(2)}) copy-start(s32[2]{0:T(128)} %constant.90) | copy-start | bytes 28
  17.2 9.7 %copy-start.11 = (s32[2]{0:T(128)S(1)}, s32[2]{0:T(128)}, u32[]{:S(2)}) copy-start(s32[2]{0:T(128)} %constant.93) | copy-start | bytes 28
  26.0 1.1 copy-start.3
  26.1 1.0 copy-start.5
  45.3 13.3 %all-to-all-start = ((bf16[8,2,2048]{2,1,0:T(2,128)(2,1)}), bf16[8,2,2048]{2,1,0:T(2,128)(2,1)S(1)}, u32[]{:S(2)}, u32[]{:S(2)}) async-start(bf16[8,2,2048]{2,1,0:T(2,128)(2,1)} %reshape.175), calls=%async_computation | async-start | bytes 131072 | tf_op jit(solution)/shard_map/all_to_all | solution.py:116
  63.9 28.0 %all-to-all-start.1 = ((bf16[8,2,4096]{2,1,0:T(2,128)(2,1)}), bf16[8,2,4096]{2,1,0:T(2,128)(2,1)S(1)}, u32[]{:S(2)}, u32[]{:S(2)}) async-start(bf16[8,2,4096]{2,1,0:T(2,128)(2,1)} %reshape.177), calls=%async_computation.1 | async-start | bytes 262144 | tf_op jit(solution)/shard_map/all_to_all | solution.py:128
  68.7 31.3 %collective-permute-start.2 = (f32[1,1,2048]{2,1,0:T(1,128)}, f32[1,1,2048]{2,1,0:T(1,128)}, u32[]{:S(2)}, u32[]{:S(2)}) collective-permute-start(f32[1,1,2048]{2,1,0:T(1,128)} %get-tuple-element.27), channel_id=1, source_target_pairs={{1,0},{2,1},{3,2},{4,3},{5,4},{6,5},{7,6},{9,8},{10,9},{11,10},{12... | collective-permute-start | bytes 24584 | tf_op jit(solution)/shard_map/ppermute | solution.py:26
  70.0 30.0 %collective-permute-start.3 = (f32[1,1,2048]{2,1,0:T(1,128)}, f32[1,1,2048]{2,1,0:T(1,128)}, u32[]{:S(2)}, u32[]{:S(2)}) collective-permute-start(f32[1,1,2048]{2,1,0:T(1,128)} %get-tuple-element.28), channel_id=1, source_target_pairs={{0,1},{1,2},{2,3},{3,4},{4,5},{5,6},{6,7},{8,9},{9,10},{10,11},{11... | collective-permute-start | bytes 24584 | tf_op jit(solution)/shard_map/ppermute | solution.py:24
  95.1 5.6 %copy-start.2 = (f32[64,2048]{1,0:T(8,128)S(1)}, f32[64,2048]{1,0:T(8,128)}, u32[]{:S(2)}) copy-start(f32[64,2048]{1,0:T(8,128)} %param.15) | copy-start | bytes 1572868
  95.6 4.4 %collective-permute-start = (f32[1,1,2048]{2,1,0:T(1,128)S(1)}, f32[1,1,2048]{2,1,0:T(1,128)S(1)}, u32[]{:S(2)}, u32[]{:S(2)}) collective-permute-start(f32[1,1,2048]{2,1,0:T(1,128)S(1)} %get-tuple-element.37), channel_id=1, source_target_pairs={{1,0},{2,1},{3,2},{4,3},{5,4},{6,5},{7,6},{9,8},{10,9},{11,10},{12... | collective-permute-start | bytes 24584 | tf_op jit(solution)/shard_map/ppermute | solution.py:26
  96.9 3.8 %collective-permute-start.1 = (f32[1,1,2048]{2,1,0:T(1,128)S(1)}, f32[1,1,2048]{2,1,0:T(1,128)S(1)}, u32[]{:S(2)}, u32[]{:S(2)}) collective-permute-start(f32[1,1,2048]{2,1,0:T(1,128)S(1)} %get-tuple-element.38), channel_id=1, source_target_pairs={{0,1},{1,2},{2,3},{3,4},{4,5},{5,6},{6,7},{8,9},{9,10},{10,11},{11... | collective-permute-start | bytes 24584 | tf_op jit(solution)/shard_map/ppermute | solution.py:24
  102.1 7.4 %copy-start.9 = (s32[2,4]{1,0:T(2,128)S(1)}, s32[2,4]{1,0:T(2,128)}, u32[]{:S(2)}) copy-start(s32[2,4]{1,0:T(2,128)} %param.23) | copy-start | bytes 100
  102.3 4.4 %collective-permute-start.4 = (f32[1,1,2048]{2,1,0:T(1,128)S(1)}, f32[1,1,2048]{2,1,0:T(1,128)S(1)}, u32[]{:S(2)}, u32[]{:S(2)}) collective-permute-start(f32[1,1,2048]{2,1,0:T(1,128)S(1)} %get-tuple-element.25), channel_id=1, source_target_pairs={{1,0},{2,1},{3,2},{4,3},{5,4},{6,5},{7,6},{9,8},{10,9},{11,10},{12... | collective-permute-start | bytes 24584 | tf_op jit(solution)/shard_map/ppermute | solution.py:26
  103.6 3.8 %collective-permute-start.5 = (f32[1,1,2048]{2,1,0:T(1,128)S(1)}, f32[1,1,2048]{2,1,0:T(1,128)S(1)}, u32[]{:S(2)}, u32[]{:S(2)}) collective-permute-start(f32[1,1,2048]{2,1,0:T(1,128)S(1)} %get-tuple-element.26), channel_id=1, source_target_pairs={{0,1},{1,2},{2,3},{3,4},{4,5},{5,6},{6,7},{8,9},{9,10},{10,11},{11... | collective-permute-start | bytes 24584 | tf_op jit(solution)/shard_map/ppermute | solution.py:24
  107.9 14.1 %collective-permute-start.6 = (f32[1,64,2048]{2,1,0:T(8,128)S(1)}, f32[1,64,2048]{2,1,0:T(8,128)S(1)}, u32[]{:S(2)}, u32[]{:S(2)}) collective-permute-start(f32[1,64,2048]{2,1,0:T(8,128)S(1)} %fusion.27), channel_id=1, source_target_pairs={{0,8},{8,0},{16,24},{24,16},{1,9},{9,1},{17,25},{25,17},{2,10},{10... | collective-permute-start | bytes 1572872 | tf_op jit(solution)/shard_map/ppermute | solution.py:36
  122.1 26.6 %collective-permute-start.7 = (f32[1,64,2048]{2,1,0:T(8,128)S(1)}, f32[1,64,2048]{2,1,0:T(8,128)S(1)}, u32[]{:S(2)}, u32[]{:S(2)}) collective-permute-start(f32[1,64,2048]{2,1,0:T(8,128)S(1)} %fusion.19), channel_id=1, source_target_pairs={{0,16},{8,24},{16,0},{24,8},{1,17},{9,25},{17,1},{25,9},{2,18},{10... | collective-permute-start | bytes 1572872 | tf_op jit(solution)/shard_map/ppermute | solution.py:36
  148.8 8.6 %copy-start.1 = (f32[1,64,2048]{2,1,0:T(8,128)}, f32[1,64,2048]{2,1,0:T(8,128)S(1)}, u32[]{:S(2)}) copy-start(f32[1,64,2048]{2,1,0:T(8,128)S(1)} %fusion.17) | copy-start | bytes 1572868
  148.8 8.7 %copy-start.4 = (f32[64,16]{1,0:T(8,128)S(1)}, f32[64,16]{1,0:T(8,128)}, u32[]{:S(2)}) copy-start(f32[64,16]{1,0:T(8,128)} %copy-done.3) | copy-start | bytes 12292
  148.8 8.7 %copy-start.6 = (f32[64,16]{1,0:T(8,128)S(1)}, f32[64,16]{1,0:T(8,128)}, u32[]{:S(2)}) copy-start(f32[64,16]{1,0:T(8,128)} %copy-done.5) | copy-start | bytes 12292
where the time goes:
time: 174 us; the launch traced here: 172 us
  other arithmetic  43.2 us (25%)
  waiting for transfers between devices  33.4 us (19%)
  blocking collectives  28.3 us (16%)
  starting transfers between devices  27.2 us (16%)
  local copies, waits for them, and re-layouts  26.2 us (15%)
  between operations  8.83 us (5%)
  matrix products  4.88 us (3%)
    ppermute x2, waiting for transfers between devices, swapped(): return lax.ppermute(value, axis, pairs)  31.9 us
    gather x5, local copies, waits for them, and re-layouts, compare_obs(): seen_vals = jnp.take_along_axis(grid_field, index_grid, axis=-1)  17.4 us
    convert_element_type x2, other arithmetic, tables(): cosines = jnp.cos(angles).astype(jnp.bfloat16)  15.4 us
    psum x1, blocking collectives, per_device(): misfit = lax.psum(misfit_part, 'space')  15 us
    psum x1, blocking collectives, per_device(): misfit_out = lax.psum(final_part, 'space')  13.3 us
    convert_element_type x2, other arithmetic, tables(): sines = jnp.sin(angles[:, 1:half_modes]).astype(jnp.bfloat16)  10.9 us
    ppermute x3, starting transfers between devices, extended(): lax.ppermute(tail, axis, [(i, (i + 1) % count) for i in range(ends)])  9.7 us
    unnamed x5, other arithmetic  7.72 us
  transfers between devices with their start and end apart: 10, of which 4 were waited for; matrix products, arithmetic and copies ran while one was open for 7% of the time, Pallas kernels for 0%

commit v1 on v0

v1 whole, which is shorter than its diff:
```python
import functools
import math

import jax
import jax.numpy as jnp
import ml_dtypes
import numpy as np
from jax import lax
from jax.experimental import pallas as pl
from jax.experimental.pallas import tpu as pltpu
from jax.sharding import PartitionSpec as P

STRETCH = 0.05
RELAX_RATE = 0.8
NOISE_AMP = 0.3
HALO = 8
PIECES = 4
MESH = pl.DeviceIdType.MESH


def tables(extent, half_modes):
    cell_index = np.arange(extent, dtype=np.int32)[:, None]
    frequency = np.arange(half_modes + 1, dtype=np.int32)[None, :]
    angles = (cell_index * frequency % extent).astype(np.float32) * np.float32(2.0 * math.pi / extent)
    cosines = np.cos(angles).astype(ml_dtypes.bfloat16)
    sines = np.sin(angles[:, 1:half_modes]).astype(ml_dtypes.bfloat16)
    return np.concatenate([cosines, sines], axis=1)


def pick(flag, yes, no):
    return jnp.where(jnp.full(yes.shape, flag, jnp.int32) > 0, yes, no)


def gather_rows(field_ref, col_ref):
    rows, columns = field_ref.shape
    obs = col_ref.shape[1]

    def block(i, seen):
        top = pl.multiple_of(i * 8, 8)
        field = field_ref[pl.ds(top, 8), :]
        cols = col_ref[pl.ds(top, 8), :]
        x_index = lax.broadcasted_iota(jnp.int32, (8, columns), 1)
        lane = lax.broadcasted_iota(jnp.int32, (8, 128), 1)
        found = jnp.zeros((8, 128), jnp.float32)
        for j in range(obs):
            hit = jnp.where(x_index == cols[:, j : j + 1], field, 0.0)
            found = jnp.where(lane == j, jnp.sum(hit, axis=1, keepdims=True), found)
        seen[pl.ds(top, 8), :] = found

    return block


def kernel(
    ns,
    npart,
    norm_factor,
    stream_ref,
    depth_ref,
    col_ref,
    val_ref,
    wgt_ref,
    lw_ref,
    target_ref,
    spec_ref,
    noise_ref,
    sel_ref,
    x_hbm,
    xt_hbm,
    yt_hbm,
    ye_hbm,
    out_ref,
    misfit_ref,
    x_tab,
    xt_tab,
    yt_tab,
    ye_tab,
    tab_sem,
    seen_ref,
    zsend,
    zrecv,
    zs_sem,
    zr_sem,
    noise_a,
    noise_mid,
    noise_b,
    ns_sem,
    nr_sem,
    buf_a,
    mid,
    buf_b,
    as_sem,
    ar_sem,
    bs_sem,
    br_sem,
    dext,
    ds_sem,
    dr_sem,
    w_ref,
    grad,
    send1,
    recv1,
    s1_sem,
    r1_sem,
    st_ref,
    send2,
    recv2,
    s2_sem,
    r2_sem,
    aux_send,
    aux_recv,
    xs_sem,
    xr_sem,
    lhs,
    d_ref,
    d2_ref,
    fin_send,
    fin_recv,
    fs_sem,
    fr_sem,
):
    rows, columns = stream_ref.shape
    obs = col_ref.shape[1]
    kl, n_modes = spec_ref.shape
    ext = rows + 2 * HALO
    me = lax.axis_index("space")
    mp = lax.axis_index("particle")
    p1 = mp + 1 - 2 * (mp % 2)
    p2 = mp + 2 - 4 * ((mp // 2) % 2)
    p3 = p1 + 2 - 4 * ((p1 // 2) % 2)
    above = (me + ns - 1) % ns
    below = (me + 1) % ns
    t0 = sel_ref[0, mp]
    t1 = sel_ref[1, mp]
    t0_far = sel_ref[0, p2]

    loads = []
    for i, (src, dst) in enumerate(((x_hbm, x_tab), (yt_hbm, yt_tab), (ye_hbm, ye_tab), (xt_hbm, xt_tab))):
        copy = pltpu.make_async_copy(src, dst, tab_sem.at[i])
        copy.start()
        loads.append(copy)

    barrier = pltpu.get_barrier_semaphore()
    for off in range(1, ns):
        pl.semaphore_signal(barrier, inc=1, device_id={"particle": mp, "space": (me + off) % ns}, device_id_type=MESH)
    for other in (p1, p2, p3):
        pl.semaphore_signal(barrier, inc=1, device_id={"particle": other, "space": me}, device_id_type=MESH)

    own_block = gather_rows(stream_ref, col_ref)

    @pl.loop(0, rows // 8)
    def _(i):
        own_block(i, seen_ref)

    wide = jnp.concatenate([seen_ref[...], jnp.zeros((128 - rows, 128), jnp.float32)], axis=0)
    zsend[0:obs, :] = wide.T[0:obs, :]
    zsend[obs : obs + 8, :] = jnp.full((8, 128), lw_ref[0], jnp.float32)

    pl.semaphore_wait(barrier, ns - 1 + 3)

    def send(src, dst, s_sem, r_sem, particle, space):
        copy = pltpu.make_async_remote_copy(
            src_ref=src,
            dst_ref=dst,
            send_sem=s_sem,
            recv_sem=r_sem,
            device_id={"particle": particle, "space": space},
            device_id_type=MESH,
        )
        copy.start()
        return copy

    z_copies = [
        send(zsend, zrecv.at[i], zs_sem.at[i], zr_sem.at[i], other, me) for i, other in enumerate((p1, p2, p3))
    ]
    na_copy = send(noise_ref, noise_a, ns_sem.at[0], nr_sem.at[0], p1, me)
    step_rows = rows // PIECES
    part = [pl.ds(i * step_rows, step_rows) for i in range(PIECES)]
    a_copies = [
        send(stream_ref.at[part[i]], buf_a.at[part[i]], as_sem.at[i], ar_sem.at[i], p1, me) for i in range(PIECES)
    ]
    d_copies = [
        send(depth_ref.at[pl.ds(rows - HALO, HALO)], dext.at[pl.ds(0, HALO)], ds_sem.at[0], dr_sem.at[0], mp, below),
        send(depth_ref.at[pl.ds(0, HALO)], dext.at[pl.ds(HALO + rows, HALO)], ds_sem.at[1], dr_sem.at[1], mp, above),
    ]
    spec_t = spec_ref[...].T

    for copy in z_copies:
        copy.wait_recv()
    near = pick(t0, zrecv[0], zsend[...])
    far = pick(t0_far, zrecv[2], zrecv[1])
    chosen = pick(t1, far, near)
    back = jnp.concatenate([chosen, jnp.zeros((128 - obs - 8, 128), jnp.float32)], axis=0).T
    seen = back[0:rows, 0:obs]
    log_weight = back[0:1, obs : obs + 1]
    miss = val_ref[...] - seen
    weighted_miss = wgt_ref[...] * miss
    misfit_part = 0.5 * jnp.sum(weighted_miss * miss, keepdims=True)
    seen_ref[...] = back[0:rows, :]

    @pl.loop(0, rows // 16)
    def _(i):
        top = pl.multiple_of(i * 16, 16)
        cols = col_ref[pl.ds(top, 16), :]
        values = wgt_ref[pl.ds(top, 16), :] * (val_ref[pl.ds(top, 16), :] - seen_ref[pl.ds(top, 16), 0:obs])
        x_index = lax.broadcasted_iota(jnp.int32, (16, columns), 1)
        total = jnp.zeros((16, columns), jnp.float32)
        for j in range(obs):
            total = total + jnp.where(x_index == cols[:, j : j + 1], values[:, j : j + 1], 0.0)
        grad[pl.ds(top, 16), :] = total.astype(jnp.bfloat16)

    loads[0].wait()
    row_modes = jnp.dot(grad[...], x_tab[...], preferred_element_type=jnp.float32)
    for j in range(ns):
        send1[j] = row_modes[:, j * kl : (j + 1) * kl].astype(jnp.bfloat16)
    mine = pl.ds(pl.multiple_of(me * rows, rows), rows)
    copies1 = []
    for off in range(1, ns):
        peer = (me + off) % ns
        copies1.append(send(send1.at[peer], recv1.at[mine], s1_sem.at[off], r1_sem.at[off], mp, peer))
    recv1[mine, :] = send1[me]

    def relay(i):
        a_copies[i].wait_recv()
        mid[part[i], :] = pick(t0, buf_a[part[i], :], stream_ref[part[i], :])
        return send(mid.at[part[i]], buf_b.at[part[i]], bs_sem.at[i], br_sem.at[i], p2, me)

    na_copy.wait_recv()
    noise_mid[...] = pick(t0, noise_a[...].astype(jnp.float32), noise_ref[...].astype(jnp.float32)).astype(jnp.bfloat16)
    nb_copy = send(noise_mid, noise_b, ns_sem.at[1], nr_sem.at[1], p2, me)
    b_copies = [relay(0)]
    shape_gain = jnp.sqrt(norm_factor * spec_ref[...])

    for copy in copies1:
        copy.wait_recv()
    loads[1].wait()
    coef = jnp.dot(yt_tab[...], recv1[...], preferred_element_type=jnp.float32)
    weighted = coef * (norm_factor * spec_t)
    energy_part = jnp.sum(coef * weighted, keepdims=True)
    st_ref[:, 0:kl] = weighted
    nb_copy.wait_recv()
    noise = pick(t1, noise_b[...].astype(jnp.float32), noise_mid[...].astype(jnp.float32))
    st_ref[:, kl : 2 * kl] = (shape_gain * noise).T
    line = lax.broadcasted_iota(jnp.int32, (8, 128), 0)
    aux_send[...] = jnp.where(line == 0, energy_part, jnp.where(line == 1, misfit_part, 0.0))
    loads[2].wait()
    send2[...] = jnp.dot(
        ye_tab[...], st_ref[...].astype(jnp.bfloat16), preferred_element_type=jnp.float32
    ).astype(jnp.bfloat16)
    copies2 = []
    for off in range(1, ns):
        peer = (me + off) % ns
        block = pl.ds(pl.multiple_of(peer * ext, 16), ext)
        copies2.append(send(send2.at[block], recv2.at[me], s2_sem.at[off], r2_sem.at[off], mp, peer))
        copies2.append(send(aux_send, aux_recv.at[me], xs_sem.at[off], xr_sem.at[off], mp, peer))
    recv2[me] = send2[pl.ds(pl.multiple_of(me * ext, 16), ext), :]
    aux_recv[me] = aux_send[...]

    for i in range(1, PIECES):
        b_copies.append(relay(i))

    for copy in d_copies:
        copy.wait_recv()
    dext[HALO : HALO + rows, :] = depth_ref[...]
    grid_row = lax.broadcasted_iota(jnp.int32, (ext, columns), 0) + (me * rows - HALO)
    inside = (grid_row >= 0) & (grid_row < ns * rows)
    w_ref[...] = jnp.where(inside, RELAX_RATE / (4.0 + STRETCH / dext[...]), 0.0)

    for copy in copies2:
        copy.wait_recv()
    for j in range(ns):
        block = recv2[j].astype(jnp.float32)
        lhs[0:ext, j * kl : (j + 1) * kl] = block[:, 0:kl]
        lhs[ext : 2 * ext, j * kl : (j + 1) * kl] = block[:, kl : 2 * kl]
    totals = aux_recv[0]
    for j in range(1, ns):
        totals = totals + aux_recv[j]
    energy = totals[0:1, 0:1]
    misfit = totals[1:2, 0:1]
    step_size = (misfit + log_weight - target_ref[0]) / (energy + 1.0)
    loads[3].wait()
    left = lhs[...].astype(jnp.bfloat16)
    width = columns // 4

    @pl.loop(0, 4)
    def _(i):
        cols = pl.ds(pl.multiple_of(i * width, width), width)
        pulled = jnp.dot(left, xt_tab[:, cols], preferred_element_type=jnp.float32)
        d_ref[:, cols] = step_size * pulled[0:ext] + NOISE_AMP * pulled[ext : 2 * ext]

    def neighbours(field):
        return (
            pltpu.roll(field, 1, 0)
            + pltpu.roll(field, ext - 1, 0)
            + pltpu.roll(field, 1, 1)
            + pltpu.roll(field, columns - 1, 1)
        )

    first = d_ref[...]
    w = w_ref[...]
    once = (1.0 - RELAX_RATE) * first + w * (neighbours(first) - first)
    twice = (1.0 - RELAX_RATE) * once + w * (neighbours(once) - first)
    d2_ref[...] = twice[HALO : HALO + rows, :]

    last_block = gather_rows(d2_ref, col_ref)
    stash = seen_ref[:, 0:obs]

    @pl.loop(0, rows // 8)
    def _(i):
        last_block(i, seen_ref)

    final_miss = val_ref[...] - (stash + seen_ref[:, 0:obs])
    final_part = 0.5 * jnp.sum(wgt_ref[...] * final_miss * final_miss, keepdims=True)
    fin_send[...] = jnp.broadcast_to(final_part, (8, 128))
    copies3 = []
    for off in range(1, ns):
        peer = (me + off) % ns
        copies3.append(send(fin_send, fin_recv.at[me], fs_sem.at[off], fr_sem.at[off], mp, peer))
    fin_recv[me] = fin_send[...]

    for i in range(PIECES):
        b_copies[i].wait_recv()
        out_ref[part[i], :] = pick(t1, buf_b[part[i], :], mid[part[i], :]) + d2_ref[part[i], :]

    for copy in copies3:
        copy.wait_recv()
    final = fin_recv[0]
    for j in range(1, ns):
        final = final + fin_recv[j]
    misfit_ref[...] = final

    for copy in z_copies + [na_copy, nb_copy] + a_copies + b_copies + d_copies + copies1 + copies2 + copies3:
        copy.wait_send()


def per_device(
    ns,
    npart,
    stream,
    depth_field,
    obs_col,
    obs_val,
    obs_weight,
    log_weight,
    target,
    spectrum,
    noise_coef,
    selection,
):
    _, rows, columns = stream.shape
    kl, n_modes = spectrum.shape
    obs = obs_col.shape[1]
    total_rows = rows * ns
    ext = rows + 2 * HALO
    x_np = tables(columns, n_modes // 2)
    y_np = tables(total_rows, n_modes // 2)
    padded = np.pad(y_np, ((HALO, HALO), (0, 0)))
    ye_np = np.concatenate([padded[j * rows : j * rows + ext] for j in range(ns)], axis=0)
    f32, bf16 = jnp.float32, jnp.bfloat16
    vmem = pl.BlockSpec(memory_space=pltpu.VMEM)
    smem = pl.BlockSpec(memory_space=pltpu.SMEM)
    hbm = pl.BlockSpec(memory_space=pl.ANY)
    dma = pltpu.SemaphoreType.DMA
    analysis, misfit = pl.pallas_call(
        functools.partial(kernel, ns, npart, 4.0 / (columns * total_rows)),
        out_shape=(jax.ShapeDtypeStruct((rows, columns), f32), jax.ShapeDtypeStruct((8, 128), f32)),
        in_specs=[vmem] * 5 + [smem, smem, vmem, vmem, smem] + [hbm] * 4,
        out_specs=(vmem, vmem),
        scratch_shapes=[
            pltpu.VMEM((columns, n_modes), bf16),
            pltpu.VMEM((n_modes, columns), bf16),
            pltpu.VMEM((n_modes, total_rows), bf16),
            pltpu.VMEM((ns * ext, n_modes), bf16),
            dma((4,)),
            pltpu.VMEM((rows, 128), f32),
            pltpu.VMEM((obs + 8, 128), f32),
            pltpu.VMEM((3, obs + 8, 128), f32),
            dma((3,)),
            dma((3,)),
            pltpu.VMEM((kl, n_modes), bf16),
            pltpu.VMEM((kl, n_modes), bf16),
            pltpu.VMEM((kl, n_modes), bf16),
            dma((2,)),
            dma((2,)),
            pltpu.VMEM((rows, columns), f32),
            pltpu.VMEM((rows, columns), f32),
            pltpu.VMEM((rows, columns), f32),
            dma((PIECES,)),
            dma((PIECES,)),
            dma((PIECES,)),
            dma((PIECES,)),
            pltpu.VMEM((ext, columns), f32),
            dma((2,)),
            dma((2,)),
            pltpu.VMEM((ext, columns), f32),
            pltpu.VMEM((rows, columns), bf16),
            pltpu.VMEM((ns, rows, kl), bf16),
            pltpu.VMEM((total_rows, kl), bf16),
            dma((ns,)),
            dma((ns,)),
            pltpu.VMEM((n_modes, 2 * kl), f32),
            pltpu.VMEM((ns * ext, 2 * kl), bf16),
            pltpu.VMEM((ns, ext, 2 * kl), bf16),
            dma((ns,)),
            dma((ns,)),
            pltpu.VMEM((8, 128), f32),
            pltpu.VMEM((ns, 8, 128), f32),
            dma((ns,)),
            dma((ns,)),
            pltpu.VMEM((2 * ext, n_modes), f32),
            pltpu.VMEM((ext, columns), f32),
            pltpu.VMEM((rows, columns), f32),
            pltpu.VMEM((8, 128), f32),
            pltpu.VMEM((ns, 8, 128), f32),
            dma((ns,)),
            dma((ns,)),
        ],
        compiler_params=pltpu.CompilerParams(
            collective_id=0, has_side_effects=True, vmem_limit_bytes=48 * 1024 * 1024
        ),
        cost_estimate=pl.CostEstimate(flops=10**9, bytes_accessed=8 * 10**6, transcendentals=0),
    )(
        stream[0],
        depth_field,
        obs_col,
        obs_val,
        obs_weight,
        log_weight,
        target,
        spectrum,
        noise_coef[0],
        selection,
        jnp.asarray(x_np),
        jnp.asarray(np.ascontiguousarray(x_np.T)),
        jnp.asarray(np.ascontiguousarray(y_np.T)),
        jnp.asarray(ye_np),
    )
    return analysis[None], misfit[0, :1]


def solution(mesh):
    return jax.shard_map(
        functools.partial(per_device, mesh.shape["space"], mesh.shape["particle"]),
        mesh=mesh,
        in_specs=(
            P("particle", "space", None),
            P("space", None),
            P("space", None),
            P("space", None),
            P("space", None),
            P("particle"),
            P(),
            P("space", None),
            P("particle", "space", None),
            P(),
        ),
        out_specs=(P("particle", "space", None), P("particle")),
        check_vma=False,
    )
```

time: 174 us -> 61.4 us (0.35)
  Pallas kernels: 0 us -> 47 us
  other arithmetic: 43.2 us -> 0 us
  waiting for transfers between devices: 33.4 us -> 0 us
  blocking collectives: 28.3 us -> 0 us
  starting transfers between devices: 27.2 us -> 0 us
  local copies, waits for them, and re-layouts: 26.2 us -> 11.9 us
  between operations: 8.83 us -> 1.94 us
  matrix products: 4.88 us -> 0 us
    pallas_call x0 -> x1, Pallas kernels: none -> 47 us  [per_device(): pl.pallas_call(functools.partial(kernel, ns, npart, 4.0 / (columns * tota...]
    ppermute x8 -> x0, waiting for transfers between devices: 33.4 us -> none  [the longest x2 31.9 us: swapped(): return lax.ppermute(value, axis, pairs)]
    psum x2 -> x0, blocking collectives: 28.3 us -> none  [the longest x1 15 us: per_device(): misfit = lax.psum(misfit_part, 'space')]
    convert_element_type x6 -> x0, other arithmetic: 28 us -> none  [the longest x2 15.4 us: tables(): cosines = jnp.cos(angles).astype(jnp.bfloat16)]
    ppermute x8 -> x0, starting transfers between devices: 17.9 us -> none  [the longest x3 9.7 us: extended(): lax.ppermute(tail, axis, [(i, (i + 1) % count) for i in range(ends)])]
    gather x5 -> x0, local copies, waits for them, and re-layouts: 17.4 us -> none  [compare_obs(): seen_vals = jnp.take_along_axis(grid_field, index_grid, axis=-1)]
    all_to_all x2 -> x0, starting transfers between devices: 9.37 us -> none  [the longest x1 5.17 us: per_device(): lax.all_to_all(row_modes, 'space', split_axis=1, concat_axis=2, tiled=True)]
    unnamed x5 -> x0, other arithmetic: 7.72 us -> none
  transfers between devices with their start and end apart: 10 -> 0, of which waited for: 4 -> 0; matrix products, arithmetic and copies ran while one was open for 7% -> 0% of each run, Pallas kernels for 0% -> 0%
where the time goes in v1:
time: 61.4 us; the launch traced here: 60.8 us
  Pallas kernels  47 us (77%)
  local copies, waits for them, and re-layouts  11.9 us (19%)
  between operations  1.94 us (3%)
    pallas_call x1, Pallas kernels, per_device(): pl.pallas_call(functools.partial(kernel, ns, npart, 4.0 / (columns * tota...  47 us
    unnamed x20, local copies, waits for them, and re-layouts  11.4 us

profile of v1, /device:TPU:0, one launch (start us, length us, event | category | flops | bytes accessed | tf_op | source)
XLA Modules:
  0.0 60.8 jit_solution(14860097493939297784)
XLA Ops:
  1.9 0.8 %copy.16.col_ref = s32[64,16]{1,0:T(8,128)S(1)} copy(s32[64,16]{0,1:T(8,128)} %param.16) | data formatting | bytes 8192 | tf_op args[2]
  2.7 0.8 %copy.17.val_ref = f32[64,16]{1,0:T(8,128)S(1)} copy(f32[64,16]{0,1:T(8,128)} %param.17) | data formatting | bytes 8192 | tf_op args[3]
  3.5 0.8 %copy.18.wgt_ref = f32[64,16]{1,0:T(8,128)S(1)} copy(f32[64,16]{0,1:T(8,128)} %param.18) | data formatting | bytes 8192 | tf_op args[4]
  4.3 0.0 copy-start
  4.3 1.6 %copy-done = bf16[2048,512]{1,0:T(8,128)(2,1)S(1)} copy-done((bf16[2048,512]{1,0:T(8,128)(2,1)S(1)}, bf16[2048,512]{1,0:T(8,128)(2,1)}, u32[]{:S(2)}) %copy-start) | copy-done | bytes 2097176
  5.9 0.0 copy-start.1
  5.9 1.1 %copy-done.1 = bf16[640,512]{1,0:T(8,128)(2,1)S(1)} copy-done((bf16[640,512]{1,0:T(8,128)(2,1)S(1)}, bf16[640,512]{1,0:T(8,128)(2,1)}, u32[]{:S(2)}) %copy-start.1) | copy-done | bytes 655384
  6.9 0.0 copy-start.2
  6.9 1.0 %copy-done.2 = f32[1,64,2048]{2,1,0:T(8,128)S(1)} copy-done((f32[1,64,2048]{2,1,0:T(8,128)S(1)}, f32[1,64,2048]{2,1,0:T(8,128)}, u32[]{:S(2)}) %copy-start.2) | copy-done | bytes 524312
  8.0 0.0 copy-start.3
  8.0 1.0 %copy-done.3 = f32[64,2048]{1,0:T(8,128)S(1)} copy-done((f32[64,2048]{1,0:T(8,128)S(1)}, f32[64,2048]{1,0:T(8,128)}, u32[]{:S(2)}) %copy-start.3) | copy-done | bytes 524312
  9.0 0.0 copy-start.4
  9.0 1.0 %copy-done.4 = bf16[512,512]{1,0:T(8,128)(2,1)S(1)} copy-done((bf16[512,512]{1,0:T(8,128)(2,1)S(1)}, bf16[512,512]{1,0:T(8,128)(2,1)}, u32[]{:S(2)}) %copy-start.4) | copy-done | bytes 524312
  10.1 0.0 copy-start.5
  10.1 0.9 %copy-done.5 = f32[64,512]{1,0:T(8,128)S(1)} copy-done((f32[64,512]{1,0:T(8,128)S(1)}, f32[64,512]{1,0:T(8,128)}, u32[]{:S(2)}) %copy-start.5) | copy-done | bytes 131096
  11.0 0.0 copy-start.6
  11.0 0.8 %copy-done.6 = bf16[1,64,512]{2,1,0:T(8,128)(2,1)S(1)} copy-done((bf16[1,64,512]{2,1,0:T(8,128)(2,1)S(1)}, bf16[1,64,512]{2,1,0:T(8,128)(2,1)}, u32[]{:S(2)}) %copy-start.6) | copy-done | bytes 65560
  11.8 0.0 copy-start.7
  11.8 0.7 %copy-done.7 = s32[2,4]{1,0:T(2,128)S(1)} copy-done((s32[2,4]{1,0:T(2,128)S(1)}, s32[2,4]{1,0:T(2,128)}, u32[]{:S(2)}) %copy-start.7) | copy-done | bytes 56
  12.5 47.0 %shard_map.149 = (f32[64,2048]{1,0:T(8,128)S(1)}, f32[8,128]{1,0:T(8,128)S(1)}) custom-call(f32[64,2048]{1,0:T(8,128)S(1)} %bitcast.4, f32[64,2048]{1,0:T(8,128)S(1)} %copy-done.3, s32[64,16]{1,0:T(8,128)S(1)} %copy.16.col_ref, f32[64,16]{1,0:T(8,128)S(1)} %copy.17.val_ref, f32[64,16]{1,0:T(8,128)S(1)} %copy.18.wgt_ref, f32[1]{0:T(128)S(6)} %copy.20.lw_ref, ...), custom_call_target="tpu_custom_call" | custom-call | flops 1000000000 | bytes 8000000 | tf_op jit(solution)/shard_map/pallas_call | solution.py:363
  59.5 0.5 slice.3
  60.0 0.8 %copy.22 = f32[1,64,2048]{2,1,0:T(8,128)} copy(f32[1,64,2048]{2,1,0:T(8,128)S(1)} %bitcast.5) | data formatting | bytes 1048576
Async XLA Ops:
  4.3 1.6 %copy-start = (bf16[2048,512]{1,0:T(8,128)(2,1)S(1)}, bf16[2048,512]{1,0:T(8,128)(2,1)}, u32[]{:S(2)}) copy-start(bf16[2048,512]{1,0:T(8,128)(2,1)} %constant.8.clone.x_hbm) | copy-start | bytes 6291460
  5.9 1.1 %copy-start.1 = (bf16[640,512]{1,0:T(8,128)(2,1)S(1)}, bf16[640,512]{1,0:T(8,128)(2,1)}, u32[]{:S(2)}) copy-start(bf16[640,512]{1,0:T(8,128)(2,1)} %constant.11.clone.ye_hbm) | copy-start | bytes 1966084
  6.9 1.0 %copy-start.2 = (f32[1,64,2048]{2,1,0:T(8,128)S(1)}, f32[1,64,2048]{2,1,0:T(8,128)}, u32[]{:S(2)}) copy-start(f32[1,64,2048]{2,1,0:T(8,128)} %param.14) | copy-start | bytes 1572868
  8.0 1.0 %copy-start.3 = (f32[64,2048]{1,0:T(8,128)S(1)}, f32[64,2048]{1,0:T(8,128)}, u32[]{:S(2)}) copy-start(f32[64,2048]{1,0:T(8,128)} %depth_ref.1) | copy-start | bytes 1572868
  9.0 1.0 %copy-start.4 = (bf16[512,512]{1,0:T(8,128)(2,1)S(1)}, bf16[512,512]{1,0:T(8,128)(2,1)}, u32[]{:S(2)}) copy-start(bf16[512,512]{1,0:T(8,128)(2,1)} %constant.10.clone.yt_hbm) | copy-start | bytes 1572868
  10.1 0.9 %copy-start.5 = (f32[64,512]{1,0:T(8,128)S(1)}, f32[64,512]{1,0:T(8,128)}, u32[]{:S(2)}) copy-start(f32[64,512]{1,0:T(8,128)} %spec_ref.1) | copy-start | bytes 393220
  11.0 0.8 %copy-start.6 = (bf16[1,64,512]{2,1,0:T(8,128)(2,1)S(1)}, bf16[1,64,512]{2,1,0:T(8,128)(2,1)}, u32[]{:S(2)}) copy-start(bf16[1,64,512]{2,1,0:T(8,128)(2,1)} %param.22) | copy-start | bytes 196612
  11.8 0.7 %copy-start.7 = (s32[2,4]{1,0:T(2,128)S(1)}, s32[2,4]{1,0:T(2,128)}, u32[]{:S(2)}) copy-start(s32[2,4]{1,0:T(2,128)} %sel_ref.1) | copy-start | bytes 100

commit v2 on v1

--- a/solution.py
+++ b/solution.py
@@ -28,18 +28,17 @@
 
 
 def pick(flag, yes, no):
-    return jnp.where(jnp.full(yes.shape, flag, jnp.int32) > 0, yes, no)
-
-
-def gather_rows(field_ref, col_ref):
+    return jnp.where(jnp.broadcast_to(flag, yes.shape) > 0, yes, no)
+
+
+def gather_rows(field_ref, col_ref, obs):
     rows, columns = field_ref.shape
-    obs = col_ref.shape[1]
 
     def block(i, seen):
         top = pl.multiple_of(i * 8, 8)
         field = field_ref[pl.ds(top, 8), :]
         cols = col_ref[pl.ds(top, 8), :]
-        x_index = lax.broadcasted_iota(jnp.int32, (8, columns), 1)
+        x_index = lax.broadcasted_iota(jnp.int32, (8, columns), 1).astype(jnp.float32)
         lane = lax.broadcasted_iota(jnp.int32, (8, 128), 1)
         found = jnp.zeros((8, 128), jnp.float32)
         for j in range(obs):
@@ -54,16 +53,16 @@
     ns,
     npart,
     norm_factor,
-    stream_ref,
-    depth_ref,
-    col_ref,
-    val_ref,
-    wgt_ref,
-    lw_ref,
-    target_ref,
-    spec_ref,
-    noise_ref,
-    sel_ref,
+    stream_hbm,
+    depth_hbm,
+    col_hbm,
+    val_hbm,
+    wgt_hbm,
+    lw_hbm,
+    target_hbm,
+    spec_hbm,
+    noise_hbm,
+    sel_hbm,
     x_hbm,
     xt_hbm,
     yt_hbm,
@@ -74,6 +73,17 @@
     xt_tab,
     yt_tab,
     ye_tab,
+    stream_ref,
+    depth_ref,
+    obs_ref,
+    val_ref,
+    wgt_ref,
+    lw_ref,
+    target_ref,
+    spec_ref,
+    noise_ref,
+    sel_ref,
+    col_ref,
     tab_sem,
     seen_ref,
     zsend,
@@ -119,7 +129,7 @@
     fr_sem,
 ):
     rows, columns = stream_ref.shape
-    obs = col_ref.shape[1]
+    obs = obs_ref.shape[0]
     kl, n_modes = spec_ref.shape
     ext = rows + 2 * HALO
     me = lax.axis_index("space")
@@ -129,15 +139,28 @@
     p3 = p1 + 2 - 4 * ((p1 // 2) % 2)
     above = (me + ns - 1) % ns
     below = (me + 1) % ns
-    t0 = sel_ref[0, mp]
-    t1 = sel_ref[1, mp]
-    t0_far = sel_ref[0, p2]
 
     loads = []
-    for i, (src, dst) in enumerate(((x_hbm, x_tab), (yt_hbm, yt_tab), (ye_hbm, ye_tab), (xt_hbm, xt_tab))):
-        copy = pltpu.make_async_copy(src, dst, tab_sem.at[i])
+    for src, dst in (
+        (stream_hbm, stream_ref),
+        (col_hbm, obs_ref),
+        (val_hbm, val_ref),
+        (wgt_hbm, wgt_ref),
+        (lw_hbm, lw_ref),
+        (sel_hbm, sel_ref),
+        (target_hbm, target_ref),
+        (x_hbm, x_tab),
+        (noise_hbm, noise_ref),
+        (spec_hbm, spec_ref),
+        (depth_hbm, depth_ref),
+        (yt_hbm, yt_tab),
+        (ye_hbm, ye_tab),
+        (xt_hbm, xt_tab),
+    ):
+        copy = pltpu.make_async_copy(src, dst, tab_sem.at[len(loads)])
         copy.start()
         loads.append(copy)
+    x_load, noise_load, spec_load, depth_load, yt_load, ye_load, xt_load = loads[7:]
 
     barrier = pltpu.get_barrier_semaphore()
     for off in range(1, ns):
@@ -145,7 +168,20 @@
     for other in (p1, p2, p3):
         pl.semaphore_signal(barrier, inc=1, device_id={"particle": other, "space": me}, device_id_type=MESH)
 
-    own_block = gather_rows(stream_ref, col_ref)
+    for copy in loads[1:7]:
+        copy.wait()
+    columns_t = obs_ref[...].astype(jnp.float32)
+    col_ref[...] = jnp.concatenate([columns_t, jnp.zeros((128 - obs, rows), jnp.float32)], axis=0).T
+    lane_p = lax.broadcasted_iota(jnp.int32, (1, npart), 1)
+
+    def flag(section, slot):
+        return jnp.sum(jnp.where(lane_p == slot, sel_ref[section : section + 1, :], 0), axis=1, keepdims=True)
+
+    t0 = flag(0, mp)
+    t1 = flag(1, mp)
+    t0_far = flag(0, p2)
+    loads[0].wait()
+    own_block = gather_rows(stream_ref, col_ref, obs)
 
     @pl.loop(0, rows // 8)
     def _(i):
@@ -153,7 +189,7 @@
 
     wide = jnp.concatenate([seen_ref[...], jnp.zeros((128 - rows, 128), jnp.float32)], axis=0)
     zsend[0:obs, :] = wide.T[0:obs, :]
-    zsend[obs : obs + 8, :] = jnp.full((8, 128), lw_ref[0], jnp.float32)
+    zsend[obs : obs + 8, :] = jnp.broadcast_to(lw_ref[...], (8, 128))
 
     pl.semaphore_wait(barrier, ns - 1 + 3)
 
@@ -172,16 +208,17 @@
     z_copies = [
         send(zsend, zrecv.at[i], zs_sem.at[i], zr_sem.at[i], other, me) for i, other in enumerate((p1, p2, p3))
     ]
-    na_copy = send(noise_ref, noise_a, ns_sem.at[0], nr_sem.at[0], p1, me)
+    na_copy = send(noise_hbm, noise_a, ns_sem.at[0], nr_sem.at[0], p1, me)
     step_rows = rows // PIECES
     part = [pl.ds(i * step_rows, step_rows) for i in range(PIECES)]
     a_copies = [
         send(stream_ref.at[part[i]], buf_a.at[part[i]], as_sem.at[i], ar_sem.at[i], p1, me) for i in range(PIECES)
     ]
     d_copies = [
-        send(depth_ref.at[pl.ds(rows - HALO, HALO)], dext.at[pl.ds(0, HALO)], ds_sem.at[0], dr_sem.at[0], mp, below),
-        send(depth_ref.at[pl.ds(0, HALO)], dext.at[pl.ds(HALO + rows, HALO)], ds_sem.at[1], dr_sem.at[1], mp, above),
+        send(depth_hbm.at[pl.ds(rows - HALO, HALO)], dext.at[pl.ds(0, HALO)], ds_sem.at[0], dr_sem.at[0], mp, below),
+        send(depth_hbm.at[pl.ds(0, HALO)], dext.at[pl.ds(HALO + rows, HALO)], ds_sem.at[1], dr_sem.at[1], mp, above),
     ]
+    spec_load.wait()
     spec_t = spec_ref[...].T
 
     for copy in z_copies:
@@ -189,26 +226,25 @@
     near = pick(t0, zrecv[0], zsend[...])
     far = pick(t0_far, zrecv[2], zrecv[1])
     chosen = pick(t1, far, near)
-    back = jnp.concatenate([chosen, jnp.zeros((128 - obs - 8, 128), jnp.float32)], axis=0).T
-    seen = back[0:rows, 0:obs]
-    log_weight = back[0:1, obs : obs + 1]
+    seen = chosen[0:obs, 0:rows]
+    log_weight = chosen[obs : obs + 1, 0:1]
     miss = val_ref[...] - seen
     weighted_miss = wgt_ref[...] * miss
     misfit_part = 0.5 * jnp.sum(weighted_miss * miss, keepdims=True)
-    seen_ref[...] = back[0:rows, :]
+    seen_ref[...] = jnp.concatenate([weighted_miss, jnp.zeros((128 - obs, rows), jnp.float32)], axis=0).T
 
     @pl.loop(0, rows // 16)
     def _(i):
         top = pl.multiple_of(i * 16, 16)
         cols = col_ref[pl.ds(top, 16), :]
-        values = wgt_ref[pl.ds(top, 16), :] * (val_ref[pl.ds(top, 16), :] - seen_ref[pl.ds(top, 16), 0:obs])
-        x_index = lax.broadcasted_iota(jnp.int32, (16, columns), 1)
+        values = seen_ref[pl.ds(top, 16), :]
+        x_index = lax.broadcasted_iota(jnp.int32, (16, columns), 1).astype(jnp.float32)
         total = jnp.zeros((16, columns), jnp.float32)
         for j in range(obs):
             total = total + jnp.where(x_index == cols[:, j : j + 1], values[:, j : j + 1], 0.0)
         grad[pl.ds(top, 16), :] = total.astype(jnp.bfloat16)
 
-    loads[0].wait()
+    x_load.wait()
     row_modes = jnp.dot(grad[...], x_tab[...], preferred_element_type=jnp.float32)
     for j in range(ns):
         send1[j] = row_modes[:, j * kl : (j + 1) * kl].astype(jnp.bfloat16)
@@ -225,6 +261,7 @@
         return send(mid.at[part[i]], buf_b.at[part[i]], bs_sem.at[i], br_sem.at[i], p2, me)
 
     na_copy.wait_recv()
+    noise_load.wait()
     noise_mid[...] = pick(t0, noise_a[...].astype(jnp.float32), noise_ref[...].astype(jnp.float32)).astype(jnp.bfloat16)
     nb_copy = send(noise_mid, noise_b, ns_sem.at[1], nr_sem.at[1], p2, me)
     b_copies = [relay(0)]
@@ -232,7 +269,7 @@
 
     for copy in copies1:
         copy.wait_recv()
-    loads[1].wait()
+    yt_load.wait()
     coef = jnp.dot(yt_tab[...], recv1[...], preferred_element_type=jnp.float32)
     weighted = coef * (norm_factor * spec_t)
     energy_part = jnp.sum(coef * weighted, keepdims=True)
@@ -242,7 +279,7 @@
     st_ref[:, kl : 2 * kl] = (shape_gain * noise).T
     line = lax.broadcasted_iota(jnp.int32, (8, 128), 0)
     aux_send[...] = jnp.where(line == 0, energy_part, jnp.where(line == 1, misfit_part, 0.0))
-    loads[2].wait()
+    ye_load.wait()
     send2[...] = jnp.dot(
         ye_tab[...], st_ref[...].astype(jnp.bfloat16), preferred_element_type=jnp.float32
     ).astype(jnp.bfloat16)
@@ -260,6 +297,7 @@
 
     for copy in d_copies:
         copy.wait_recv()
+    depth_load.wait()
     dext[HALO : HALO + rows, :] = depth_ref[...]
     grid_row = lax.broadcasted_iota(jnp.int32, (ext, columns), 0) + (me * rows - HALO)
     inside = (grid_row >= 0) & (grid_row < ns * rows)
@@ -276,8 +314,8 @@
         totals = totals + aux_recv[j]
     energy = totals[0:1, 0:1]
     misfit = totals[1:2, 0:1]
-    step_size = (misfit + log_weight - target_ref[0]) / (energy + 1.0)
-    loads[3].wait()
+    step_size = (misfit + log_weight - target_ref[...]) / (energy + 1.0)
+    xt_load.wait()
     left = lhs[...].astype(jnp.bfloat16)
     width = columns // 4
 
@@ -301,14 +339,14 @@
     twice = (1.0 - RELAX_RATE) * once + w * (neighbours(once) - first)
     d2_ref[...] = twice[HALO : HALO + rows, :]
 
-    last_block = gather_rows(d2_ref, col_ref)
-    stash = seen_ref[:, 0:obs]
+    last_block = gather_rows(d2_ref, col_ref, obs)
 
     @pl.loop(0, rows // 8)
     def _(i):
         last_block(i, seen_ref)
 
-    final_miss = val_ref[...] - (stash + seen_ref[:, 0:obs])
+    moved = jnp.concatenate([seen_ref[...], jnp.zeros((128 - rows, 128), jnp.float32)], axis=0).T[0:obs, 0:rows]
+    final_miss = val_ref[...] - (seen + moved)
     final_part = 0.5 * jnp.sum(wgt_ref[...] * final_miss * final_miss, keepdims=True)
     fin_send[...] = jnp.broadcast_to(final_part, (8, 128))
     copies3 = []
@@ -357,20 +395,30 @@
     ye_np = np.concatenate([padded[j * rows : j * rows + ext] for j in range(ns)], axis=0)
     f32, bf16 = jnp.float32, jnp.bfloat16
     vmem = pl.BlockSpec(memory_space=pltpu.VMEM)
-    smem = pl.BlockSpec(memory_space=pltpu.SMEM)
     hbm = pl.BlockSpec(memory_space=pl.ANY)
     dma = pltpu.SemaphoreType.DMA
     analysis, misfit = pl.pallas_call(
         functools.partial(kernel, ns, npart, 4.0 / (columns * total_rows)),
         out_shape=(jax.ShapeDtypeStruct((rows, columns), f32), jax.ShapeDtypeStruct((8, 128), f32)),
-        in_specs=[vmem] * 5 + [smem, smem, vmem, vmem, smem] + [hbm] * 4,
+        in_specs=[hbm] * 14,
         out_specs=(vmem, vmem),
         scratch_shapes=[
             pltpu.VMEM((columns, n_modes), bf16),
             pltpu.VMEM((n_modes, columns), bf16),
             pltpu.VMEM((n_modes, total_rows), bf16),
             pltpu.VMEM((ns * ext, n_modes), bf16),
-            dma((4,)),
+            pltpu.VMEM((rows, columns), f32),
+            pltpu.VMEM((rows, columns), f32),
+            pltpu.VMEM((obs, rows), jnp.int32),
+            pltpu.VMEM((obs, rows), f32),
+            pltpu.VMEM((obs, rows), f32),
+            pltpu.VMEM((1, 1), f32),
+            pltpu.VMEM((1, 1), f32),
+            pltpu.VMEM((kl, n_modes), f32),
+            pltpu.VMEM((kl, n_modes), bf16),
+            pltpu.VMEM(selection.shape, jnp.int32),
+            pltpu.VMEM((rows, 128), f32),
+            dma((14,)),
             pltpu.VMEM((rows, 128), f32),
             pltpu.VMEM((obs + 8, 128), f32),
             pltpu.VMEM((3, obs + 8, 128), f32),
@@ -415,17 +463,17 @@
             dma((ns,)),
         ],
         compiler_params=pltpu.CompilerParams(
-            collective_id=0, has_side_effects=True, vmem_limit_bytes=48 * 1024 * 1024
+            collective_id=0, has_side_effects=True, vmem_limit_bytes=60 * 1024 * 1024
         ),
         cost_estimate=pl.CostEstimate(flops=10**9, bytes_accessed=8 * 10**6, transcendentals=0),
     )(
         stream[0],
         depth_field,
-        obs_col,
-        obs_val,
-        obs_weight,
-        log_weight,
-        target,
+        obs_col.T,
+        obs_val.T,
+        obs_weight.T,
+        log_weight.reshape(1, 1),
+        target.reshape(1, 1),
         spectrum,
         noise_coef[0],
         selection,

time: 61.4 us -> 53.1 us (0.86)
  local copies, waits for them, and re-layouts: 11.9 us -> 3.06 us
  Pallas kernels: 47 us -> 47.9 us
    unnamed x20 -> x1, local copies, waits for them, and re-layouts: 11.4 us -> 1.87 us
    pallas_call x1, Pallas kernels: 47 us -> 47.9 us  [per_device(): pl.pallas_call(functools.partial(kernel, ns, npart, 4.0 / (columns * tota...]
    slice x1, local copies, waits for them, and re-layouts: 0.51 us -> 1.19 us  [per_device(): return (analysis[None], misfit[0, :1])]
where the time goes in v2:
time: 53.1 us; the launch traced here: 52.9 us
  Pallas kernels  47.9 us (90%)
  local copies, waits for them, and re-layouts  3.06 us (6%)
  between operations  1.93 us (4%)
    pallas_call x1, Pallas kernels, per_device(): pl.pallas_call(functools.partial(kernel, ns, npart, 4.0 / (columns * tota...  47.9 us
    unnamed x1, local copies, waits for them, and re-layouts  1.87 us
    slice x1, local copies, waits for them, and re-layouts, per_device(): return (analysis[None], misfit[0, :1])  1.19 us

profile of v2, /device:TPU:0, one launch (start us, length us, event | category | flops | bytes accessed | tf_op | source)
XLA Modules:
  0.0 52.9 jit_solution(11863243737242854854)
XLA Ops:
  1.9 47.9 %shard_map.149 = (f32[64,2048]{1,0:T(8,128)}, f32[8,128]{1,0:T(8,128)}) custom-call(f32[64,2048]{1,0:T(8,128)} %bitcast.11, f32[64,2048]{1,0:T(8,128)} %depth_hbm.1, s32[16,64]{1,0:T(8,128)} %bitcast.14, f32[16,64]{1,0:T(8,128)} %bitcast.15, f32[16,64]{1,0:T(8,128)} %bitcast.16, f32[1,1]{1,0:T(1,128)} %bitcast.9.lw_hbm, f32[1,1]{1,0:T(1,128)} %bitcast.10.target_hbm, ...), custom_call_target="tpu_custom_call" | custom-call | flops 1000000000 | bytes 8000000 | tf_op jit(solution)/shard_map/pallas_call | solution.py:400
  49.8 1.2 %slice.3 = f32[1,1]{1,0:T(1,128)} slice(f32[8,128]{1,0:T(8,128)} %get-tuple-element.5), slice={[0:1], [0:1]} | slice | bytes 8 | tf_op jit(solution)/shard_map/slice | solution.py:485
  51.0 1.9 %copy.19 = f32[1,64,2048]{2,1,0:T(8,128)} copy(f32[1,64,2048]{2,1,0:T(8,128)} %bitcast.12) | data formatting | bytes 1048576

commit v3 on v2

--- a/solution.py
+++ b/solution.py
@@ -15,6 +15,8 @@
 NOISE_AMP = 0.3
 HALO = 8
 PIECES = 4
+CODE_SCALE = 256.0
+CODE_LEAST = 2.0**-126
 MESH = pl.DeviceIdType.MESH
 
 
@@ -29,6 +31,18 @@
 
 def pick(flag, yes, no):
     return jnp.where(jnp.broadcast_to(flag, yes.shape) > 0, yes, no)
+
+
+def coded(value):
+    scaled = value * CODE_SCALE
+    sixth = (scaled * scaled * scaled) * (scaled * scaled * scaled)
+    power = sixth * sixth
+    return jnp.where(value < 0.0, -power, power).astype(jnp.bfloat16)
+
+
+def decoded(code):
+    size = jnp.exp2(jnp.log2(jnp.maximum(jnp.abs(code), CODE_LEAST)) * (1.0 / 12.0)) * (1.0 / CODE_SCALE)
+    return jnp.where(code < 0.0, -size, size)
 
 
 def gather_rows(field_ref, col_ref, obs):
@@ -95,6 +109,7 @@
     noise_b,
     ns_sem,
     nr_sem,
+    code,
     buf_a,
     mid,
     buf_b,
@@ -211,8 +226,9 @@
     na_copy = send(noise_hbm, noise_a, ns_sem.at[0], nr_sem.at[0], p1, me)
     step_rows = rows // PIECES
     part = [pl.ds(i * step_rows, step_rows) for i in range(PIECES)]
+    code[...] = coded(stream_ref[...])
     a_copies = [
-        send(stream_ref.at[part[i]], buf_a.at[part[i]], as_sem.at[i], ar_sem.at[i], p1, me) for i in range(PIECES)
+        send(code.at[part[i]], buf_a.at[part[i]], as_sem.at[i], ar_sem.at[i], p1, me) for i in range(PIECES)
     ]
     d_copies = [
         send(depth_hbm.at[pl.ds(rows - HALO, HALO)], dext.at[pl.ds(0, HALO)], ds_sem.at[0], dr_sem.at[0], mp, below),
@@ -257,7 +273,9 @@
 
     def relay(i):
         a_copies[i].wait_recv()
-        mid[part[i], :] = pick(t0, buf_a[part[i], :], stream_ref[part[i], :])
+        mid[part[i], :] = pick(
+            t0, buf_a[part[i], :].astype(jnp.float32), code[part[i], :].astype(jnp.float32)
+        ).astype(jnp.bfloat16)
         return send(mid.at[part[i]], buf_b.at[part[i]], bs_sem.at[i], br_sem.at[i], p2, me)
 
     na_copy.wait_recv()
@@ -357,7 +375,8 @@
 
     for i in range(PIECES):
         b_copies[i].wait_recv()
-        out_ref[part[i], :] = pick(t1, buf_b[part[i], :], mid[part[i], :]) + d2_ref[part[i], :]
+        came = pick(t1, buf_b[part[i], :].astype(jnp.float32), mid[part[i], :].astype(jnp.float32))
+        out_ref[part[i], :] = pick(t0 + t1, decoded(came), stream_ref[part[i], :]) + d2_ref[part[i], :]
 
     for copy in copies3:
         copy.wait_recv()
@@ -429,9 +448,10 @@
             pltpu.VMEM((kl, n_modes), bf16),
             dma((2,)),
             dma((2,)),
-            pltpu.VMEM((rows, columns), f32),
-            pltpu.VMEM((rows, columns), f32),
-            pltpu.VMEM((rows, columns), f32),
+            pltpu.VMEM((rows, columns), bf16),
+            pltpu.VMEM((rows, columns), bf16),
+            pltpu.VMEM((rows, columns), bf16),
+            pltpu.VMEM((rows, columns), bf16),
             dma((PIECES,)),
             dma((PIECES,)),
             dma((PIECES,)),

time: 53.1 us -> 41.6 us (0.78)
  Pallas kernels: 47.9 us -> 36.4 us
    pallas_call x1, Pallas kernels: 47.9 us -> 36.4 us  [per_device(): pl.pallas_call(functools.partial(kernel, ns, npart, 4.0 / (columns * tota...]
where the time goes in v3:
time: 41.6 us; the launch traced here: 41.4 us
  Pallas kernels  36.4 us (88%)
  local copies, waits for them, and re-layouts  3.06 us (7%)
  between operations  1.93 us (5%)
    pallas_call x1, Pallas kernels, per_device(): pl.pallas_call(functools.partial(kernel, ns, npart, 4.0 / (columns * tota...  36.4 us
    unnamed x1, local copies, waits for them, and re-layouts  1.87 us
    slice x1, local copies, waits for them, and re-layouts, per_device(): return (analysis[None], misfit[0, :1])  1.19 us

profile of v3, /device:TPU:0, one launch (start us, length us, event | category | flops | bytes accessed | tf_op | source)
XLA Modules:
  0.0 41.4 jit_solution(16273288144378381686)
XLA Ops:
  1.9 36.4 %shard_map.149 = (f32[64,2048]{1,0:T(8,128)}, f32[8,128]{1,0:T(8,128)}) custom-call(f32[64,2048]{1,0:T(8,128)} %bitcast.11, f32[64,2048]{1,0:T(8,128)} %depth_hbm.1, s32[16,64]{1,0:T(8,128)} %bitcast.14, f32[16,64]{1,0:T(8,128)} %bitcast.15, f32[16,64]{1,0:T(8,128)} %bitcast.16, f32[1,1]{1,0:T(1,128)} %bitcast.9.lw_hbm, f32[1,1]{1,0:T(1,128)} %bitcast.10.target_hbm, ...), custom_call_target="tpu_custom_call" | custom-call | flops 1000000000 | bytes 8000000 | tf_op jit(solution)/shard_map/pallas_call | solution.py:419
  38.4 1.2 %slice.3 = f32[1,1]{1,0:T(1,128)} slice(f32[8,128]{1,0:T(8,128)} %get-tuple-element.5), slice={[0:1], [0:1]} | slice | bytes 8 | tf_op jit(solution)/shard_map/slice | solution.py:505
  39.5 1.9 %copy.19 = f32[1,64,2048]{2,1,0:T(8,128)} copy(f32[1,64,2048]{2,1,0:T(8,128)} %bitcast.12) | data formatting | bytes 1048576
